TPU v7x, 512 devices: a whole 4x4x16 slice. The times are simulated.
512 devices in a mesh: row: 32 (over y, x, core), col: 16 (over z).
Axes of the slice: x: 4, y: 4, z: 16, core: 2. Of those that a mesh axis runs over, the one named last changes fastest.
Arguments:
- col_samples: float32 [64, 2, 2048, 128], P('row', None, 'col'), may hold values from -6 to 6
- row_samples: float32 [64, 2, 128, 2048], P('row', None, None, 'col'), may hold values from -6 to 6
- pivot_rows: int32 [64, 128], P('row'), may hold values from 0 to 2047
- rank_blocks: int32 [64], P('row'), may hold values from 1 to 8
- upper_inverse: float32 [2, 2048, 2048], P(None, 'col', 'row'), as said below
- upanel_left: float32 [16, 2, 2048, 128], P('col'), may hold values from -0.125 to 0.125
Outputs:
- panel_right: float32 [64, 2, 128, 2048], P('row', None, None, 'col')
- cores: float32 [64, 16, 2, 128, 128], P('row', 'col')
Inputs may be any that keep to these rules, and one draw needn't show every extreme that they name: `rank_blocks`: the tile's rank is 16 times this. `upper_inverse`: zero below the diagonal in both parts.
All inputs are finite; a program needn't handle non-finite values.
Results may differ from a plain program's by a relative error of at most 0.00007.
Values sent between devices are 32-bit elements; how exact they have to be, the bound alone decides.
No kernel may reach another device: no remote copies, remote signals or barrier semaphores. Data moves between devices by JAX's collectives and lax.ppermute only.
A program may use at most 64 MiB of HBM per device.

v0:
```python
import jax
import jax.numpy as jnp
from jax import lax
from jax.sharding import PartitionSpec as P

RANK_STEP = 16


def complex_product(pattern, left_real, left_imag, right_real, right_imag):

    def single(left, right):
        return jnp.einsum(
            pattern,
            left,
            right,
            precision=lax.Precision.HIGHEST,
            preferred_element_type=jnp.float32,
        )

    real_part = single(left_real, right_real) - single(left_imag, right_imag)
    imag_part = single(left_real, right_imag) + single(left_imag, right_real)
    return (real_part, imag_part)


def scale_rows(values, weight_real, weight_imag):
    wr = weight_real[:, :, None]
    wi = weight_imag[:, :, None]
    real_part = values[:, 0] * wr - values[:, 1] * wi
    imag_part = values[:, 0] * wi + values[:, 1] * wr
    return jnp.stack((real_part, imag_part), axis=1)


def on_device(col_samples, row_samples, pivot_rows, rank_blocks, upper_inverse, upanel_left):
    width_local = col_samples.shape[2]
    ranks_max = row_samples.shape[2]
    offset = lax.axis_index("col") * width_local
    positions = offset + lax.broadcasted_iota(jnp.int32, (1, 1, width_local), 2)
    hits = (pivot_rows[:, :, None] == positions).astype(jnp.float32)
    flipped = jnp.swapaxes(col_samples, 2, 3)
    partial_entries = jnp.sum(flipped * hits[:, None], axis=3)
    entries = lax.psum(partial_entries, "col")
    levels = lax.broadcasted_iota(jnp.int32, (1, ranks_max), 1)
    keeping = (levels < RANK_STEP * rank_blocks[:, None]).astype(jnp.float32)
    magnitude = jnp.maximum(entries[:, 0] * entries[:, 0] + entries[:, 1] * entries[:, 1], 1.0)
    factor_real = keeping * entries[:, 0] / magnitude
    factor_imag = -keeping * entries[:, 1] / magnitude
    scaled = scale_rows(row_samples, factor_real, factor_imag)
    portion = lax.all_gather(upper_inverse, "row", axis=2, tiled=True)
    real_part, imag_part = complex_product(
        "trk,kn->trn", scaled[:, 0], scaled[:, 1], portion[0], portion[1]
    )
    partial_panel = jnp.stack((real_part, imag_part), axis=1)
    panel_local = lax.psum_scatter(partial_panel, "col", scatter_dimension=3, tiled=True)
    portion = lax.all_gather(panel_local, "col", axis=3, tiled=True)
    core_real, core_imag = complex_product(
        "trn,jns->tjrs", portion[:, 0], portion[:, 1], upanel_left[:, 0], upanel_left[:, 1]
    )
    cores = jnp.stack((core_real, core_imag), axis=2)
    return (panel_local, cores)


def solution(mesh):
    in_specs = (
        P("row", None, "col", None),
        P("row", None, None, "col"),
        P("row", None),
        P("row"),
        P(None, "col", "row"),
        P("col", None, None, None),
    )
    out_specs = (P("row", None, None, "col"), P("row", "col", None, None, None))
    return jax.shard_map(
        on_device, mesh=mesh, in_specs=in_specs, out_specs=out_specs, check_vma=False
    )
```

profile of v0, /device:TPU:2, one launch (start us, length us, event | category | flops | bytes accessed | tf_op | source)
XLA Modules:
  0.0 281.9 jit_solution(7301261295972462733)
XLA Ops:
  7.2 0.0 all-gather.3.cloned.1.call-start
  7.2 1.5 copy.12
  8.7 0.0 all-gather.3.cloned.1.call-update
  8.8 0.0 reduce-scatter.2.cloned.1.call-start
  8.8 0.8 compare_convert_fusion
  9.6 1.0 fusion.18
  10.6 36.5 %psum.7 = f32[2,2,128]{2,1,0:T(2,128)S(1)} all-reduce(f32[2,2,128]{2,1,0:T(2,128)S(1)} %fusion.18), channel_id=1, replica_groups=mesh['row'=32,'col'=16] {'col'}, use_global_device_ids=true, to_apply=%region_1.0 | all-reduce | flops 512 | bytes 4096 | tf_op jit(solution)/shard_map/psum | solution.py:41
  47.1 0.7 broadcast_multiply_fusion
  47.8 0.1 select_divide_fusion
  47.8 0.0 copy-start.2
  47.8 27.1 %all-gather.3.cloned.1.call-done = f32[2,128,2048]{1,0,2:T(2,128)} async-done(((f32[2,128,64]{1,0,2:T(2,128)}), f32[2,128,2048]{1,0,2:T(2,128)}) %all-gather.3.cloned.1.call-update) | async-done | bytes 2097168 | tf_op jit(solution)/shard_map/all_gather | solution.py:48
  74.9 4.0 %fusion.25 = (f32[1,128,2048]{1,0,2:T(1,128)S(1)}, f32[1,128,2048]{1,0,2:T(1,128)S(1)}) fusion(f32[2,128,2048]{1,0,2:T(2,128)} %all-gather.3.cloned.1.call-done), kind=kLoop, calls=%fused_computation.41 | loop fusion | bytes 4194304 | tf_op jit(solution)/shard_map/slice | solution.py:50
  78.9 0.0 copy-done.2
  78.9 1.8 fusion.21
  80.8 1.8 fusion.23
  82.6 1.9 fusion
  84.5 1.9 fusion.1
  86.4 2.2 pad_maximum_fusion
  88.6 0.0 copy-start.1
  88.6 0.0 reduce-scatter.2.cloned.1.call-update
  88.7 0.2 all-gather.5.cloned.1.call-start
  88.9 79.6 %reduce-scatter.2.cloned.1.call-done = f32[2,2,128,128]{3,2,0,1:T(8,128)} async-done(((f32[2,2,128,2048]{3,2,0,1:T(8,128)}), f32[2,2,128,128]{3,2,0,1:T(8,128)}) %reduce-scatter.2.cloned.1.call-update) | async-done | bytes 262160 | tf_op jit(solution)/shard_map/reduce_scatter | solution.py:53
  168.5 0.0 all-gather.5.cloned.1.call-update
  168.5 1.7 copy.15
  170.2 93.8 %all-gather.5.cloned.1.call-done = f32[2,2,128,2048]{3,2,0,1:T(8,128)} async-done(((f32[2,2,128,128]{3,2,0,1:T(8,128)}), f32[2,2,128,2048]{3,2,0,1:T(8,128)}) %all-gather.5.cloned.1.call-update) | async-done | bytes 4194320 | tf_op jit(solution)/shard_map/all_gather | solution.py:54
  263.9 0.0 copy-done.1
  263.9 0.0 copy-start
  263.9 3.6 %fusion.2 = f32[2,128,128]{2,1,0:T(8,128)S(1)} fusion(f32[2,2,128,2048]{3,2,0,1:T(8,128)} %all-gather.5.cloned.1.call-done, f32[1,2,2048,128]{3,2,1,0:T(8,128)S(1)} %copy-done.1), kind=kOutput, calls=%fused_computation.7 | convolution fusion | flops 805306368 | bytes 3276800 | tf_op jit(solution)/shard_map/trn,jns->tjrs/dot_general | solution.py:12
  267.5 3.4 %fusion.3 = f32[2,128,128]{2,1,0:T(8,128)S(1)} fusion(f32[2,2,128,2048]{3,2,0,1:T(8,128)} %all-gather.5.cloned.1.call-done, f32[1,2,2048,128]{3,2,1,0:T(8,128)S(1)} %copy-done.1), kind=kOutput, calls=%fused_computation.8 | convolution fusion | flops 805306368 | bytes 3276800 | tf_op jit(solution)/shard_map/trn,jns->tjrs/dot_general | solution.py:12
  270.9 0.0 copy-done
  270.9 1.8 fusion.9
  272.8 1.8 fusion.7
  274.6 0.7 copy.16
  (3 shorter events, 0.0 us)
Async XLA Ops:
  7.2 67.7 %all-gather.3.cloned.1.call-start = ((), (), s32[]{:S(2)}) async-start(), calls=%async_computation.1 | async-start | bytes 2162688 | tf_op jit(solution)/shard_map/all_gather | solution.py:48
  8.8 159.7 %reduce-scatter.2.cloned.1.call-start = ((), (), s32[]{:S(2)}) async-start(), calls=%async_computation.2 | async-start | bytes 4456448 | tf_op jit(solution)/shard_map/reduce_scatter | solution.py:53
  47.8 31.1 %copy-start.2 = (f32[2,2,128,128]{3,2,1,0:T(8,128)S(1)}, f32[2,2,128,128]{3,2,1,0:T(8,128)}, u32[]{:S(2)}) copy-start(f32[2,2,128,128]{3,2,1,0:T(8,128)} %param.7) | copy-start | bytes 786436
  88.6 175.3 %copy-start.1 = (f32[1,2,2048,128]{3,2,1,0:T(8,128)S(1)}, f32[1,2,2048,128]{3,2,1,0:T(8,128)}, u32[]{:S(2)}) copy-start(f32[1,2,2048,128]{3,2,1,0:T(8,128)} %param.11) | copy-start | bytes 6291460
  88.7 175.3 %all-gather.5.cloned.1.call-start = ((), (), s32[]{:S(2)}) async-start(), calls=%async_computation.3 | async-start | bytes 4456448 | tf_op jit(solution)/shard_map/all_gather | solution.py:54
  263.9 7.0 %copy-start = (f32[2,2,128,2048]{3,2,0,1:T(8,128)S(1)}, f32[2,2,128,2048]{3,2,0,1:T(8,128)}, u32[]{:S(2)}) copy-start(f32[2,2,128,2048]{3,2,0,1:T(8,128)} %all-gather.5.cloned.1.call-done) | copy-start | bytes 12582916
Sparse Core Ops, SparseCore 0:
  11.7 63.1 all-gather.2
  88.8 79.6 reduce-scatter.1
  170.5 93.4 all-gather.4
where the time goes:
time: 282 us
  waiting for transfers between devices  200 us (71%)
  blocking collectives  36.5 us (13%)
  matrix products  18.1 us (6%)
  between operations  13.9 us (5%)
  local copies, waits for them, and re-layouts  7.92 us (3%)
  other arithmetic  4.73 us (2%)
    all_gather x1, waiting for transfers between devices, on_device(): portion = lax.all_gather(panel_local, 'col', axis=3, tiled=True)  93.8 us
    reduce_scatter x1, waiting for transfers between devices, on_device(): lax.psum_scatter(partial_panel, 'col', scatter_dimension=3, tiled=True)  79.6 us
    psum x1, blocking collectives, on_device(): entries = lax.psum(partial_entries, 'col')  36.5 us
    all_gather x1, waiting for transfers between devices, on_device(): portion = lax.all_gather(upper_inverse, 'row', axis=2, tiled=True)  27.1 us
    dot_general x8, matrix products, single(): jnp.einsum(pattern, left, right, precision=lax.Precision.HIGHEST, preferr...  18.1 us
  transfers between devices with their start and end apart: 3, of which 3 were waited for; matrix products, arithmetic and copies ran while one was open for 1% of the time, Pallas kernels for 0%

commit v1 on v0

--- a/solution.py
+++ b/solution.py
@@ -2,6 +2,7 @@
 import jax.numpy as jnp
 from jax import lax
 from jax.sharding import PartitionSpec as P
+from jax.lax import axis_index, axis_size, ppermute
 
 RANK_STEP = 16
 
@@ -51,7 +52,24 @@
     )
     partial_panel = jnp.stack((real_part, imag_part), axis=1)
     panel_local = lax.psum_scatter(partial_panel, "col", scatter_dimension=3, tiled=True)
-    portion = lax.all_gather(panel_local, "col", axis=3, tiled=True)
+    f_next = axis_size("col")
+    v1, latest, z2 = (f_next, axis_index("col"), panel_local.shape[3])
+    row_list = [(pp, (pp + 1) % v1) for pp in range(v1)]
+    copies = [(pp, (pp - 1) % v1) for pp in range(v1)]
+    portion = jnp.zeros(
+        (*panel_local.shape[:3], v1 * z2, *panel_local.shape[4:]), panel_local.dtype
+    )
+    portion = lax.dynamic_update_slice_in_dim(portion, panel_local, latest * z2, axis=3)
+    z = shaped = panel_local
+    val = v1 // 2
+    for dev_j in tuple(range(1, val + 1)):
+        z = ppermute(z, perm=row_list, axis_name="col")
+        portion = lax.dynamic_update_slice_in_dim(portion, z, (latest - dev_j) % v1 * z2, axis=3)
+        if dev_j < v1 - val:
+            shaped = ppermute(shaped, axis_name="col", perm=copies)
+            portion = lax.dynamic_update_slice_in_dim(
+                portion, shaped, (latest + dev_j) % v1 * z2, axis=3
+            )
     core_real, core_imag = complex_product(
         "trn,jns->tjrs", portion[:, 0], portion[:, 1], upanel_left[:, 0], upanel_left[:, 1]
     )

time: 282 us -> 264 us (0.936)
  the two profiles are of different devices: /device:TPU:2 before, /device:TPU:6 now
where the time goes in v1:
time: 264 us
  waiting for transfers between devices  132 us (50%)
  starting transfers between devices  52.5 us (20%)
  blocking collectives  36.5 us (14%)
  matrix products  14.8 us (6%)
  between operations  14.7 us (6%)
  local copies, waits for them, and re-layouts  8.02 us (3%)
  other arithmetic  4.74 us (2%)
    reduce_scatter x1, waiting for transfers between devices, on_device(): lax.psum_scatter(partial_panel, 'col', scatter_dimension=3, tiled=True)  80.4 us
    psum x1, blocking collectives, on_device(): entries = lax.psum(partial_entries, 'col')  36.5 us
    ppermute x7, starting transfers between devices, on_device(): shaped = ppermute(shaped, axis_name='col', perm=copies)  36.4 us
    all_gather x1, waiting for transfers between devices, on_device(): portion = lax.all_gather(upper_inverse, 'row', axis=2, tiled=True)  27 us
    ppermute x8, waiting for transfers between devices, on_device(): z = ppermute(z, perm=row_list, axis_name='col')  23.2 us
    ppermute x8, starting transfers between devices, on_device(): z = ppermute(z, perm=row_list, axis_name='col')  16.1 us
    dot_general x8, matrix products, single(): jnp.einsum(pattern, left, right, precision=lax.Precision.HIGHEST, preferr...  14.8 us
  transfers between devices with their start and end apart: 17, of which 12 were waited for; matrix products, arithmetic and copies ran while one was open for 2% of the time, Pallas kernels for 0%

profile of v1, /device:TPU:6, one launch (start us, length us, event | category | flops | bytes accessed | tf_op | source)
XLA Modules:
  0.0 263.7 jit_solution(9033981773858250884)
XLA Ops:
  7.2 0.0 all-gather.2.cloned.1.call-start
  7.2 1.6 copy.12
  8.8 0.0 reduce-scatter.2.cloned.1.call-start
  8.9 0.8 compare_convert_fusion
  9.6 1.0 fusion.18
  10.6 36.5 %psum.7 = f32[2,2,128]{2,1,0:T(2,128)S(1)} all-reduce(f32[2,2,128]{2,1,0:T(2,128)S(1)} %fusion.18), channel_id=1, replica_groups=mesh['row'=32,'col'=16] {'col'}, use_global_device_ids=true, to_apply=%region_1.0 | all-reduce | flops 512 | bytes 4096 | tf_op jit(solution)/shard_map/psum | solution.py:42
  47.1 0.7 broadcast_multiply_fusion
  47.8 0.1 select_divide_fusion
  47.9 27.0 %all-gather.2.cloned.1.call-done = f32[2,128,2048]{1,0,2:T(2,128)} async-done(((f32[2,128,64]{1,0,2:T(2,128)}), f32[2,128,2048]{1,0,2:T(2,128)}) %all-gather.2.cloned.1.call-update) | async-done | bytes 2097168 | tf_op jit(solution)/shard_map/all_gather | solution.py:49
  74.9 4.1 %fusion.25 = (f32[1,128,2048]{1,0,2:T(1,128)S(1)}, f32[1,128,2048]{1,0,2:T(1,128)S(1)}) fusion(f32[2,128,2048]{1,0,2:T(2,128)} %all-gather.2.cloned.1.call-done), kind=kLoop, calls=%fused_computation.57 | loop fusion | bytes 4194304 | tf_op jit(solution)/shard_map/slice | solution.py:51
  78.9 1.8 fusion.23
  80.8 1.8 fusion.21
  82.6 1.9 fusion.1
  84.5 1.9 fusion
  86.4 2.2 pad_maximum_fusion
  88.7 80.4 %reduce-scatter.2.cloned.1.call-done = f32[2,2,128,128]{3,2,0,1:T(8,128)} async-done(((f32[2,2,128,2048]{3,2,0,1:T(8,128)}), f32[2,2,128,128]{3,2,0,1:T(8,128)}) %reduce-scatter.2.cloned.1.call-update) | async-done | bytes 262160 | tf_op jit(solution)/shard_map/reduce_scatter | solution.py:54
  169.1 2.5 collective-permute-start
  171.6 4.7 %collective-permute-start.1 = (f32[2,2,128,128]{3,2,0,1:T(8,128)}, f32[2,2,128,128]{3,2,0,1:T(8,128)S(1)}, u32[]{:S(2)}, u32[]{:S(2)}) collective-permute-start(f32[2,2,128,128]{3,2,0,1:T(8,128)} %reduce-scatter.2.cloned.1.call-done), channel_id=1, source_target_pairs={{0,15},{1,0},{2,1},{3,2},{4,3},{5,4},{6,5},{7,6},{8,7},{9,8},{10,9... | collective-permute-start | bytes 786440 | tf_op jit(solution)/shard_map/ppermute | solution.py:69
  176.3 3.4 %collective-permute-done = f32[2,2,128,128]{3,2,0,1:T(8,128)S(1)} collective-permute-done((f32[2,2,128,128]{3,2,0,1:T(8,128)}, f32[2,2,128,128]{3,2,0,1:T(8,128)S(1)}, u32[]{:S(2)}, u32[]{:S(2)}) %collective-permute-start) | collective-permute-done | bytes 262176 | tf_op jit(solution)/shard_map/ppermute | solution.py:66
  179.7 1.9 collective-permute-start.2
  181.6 5.1 %collective-permute-start.3 = (f32[2,2,128,128]{3,2,0,1:T(8,128)S(1)}, f32[2,2,128,128]{3,2,0,1:T(8,128)S(1)}, u32[]{:S(2)}, u32[]{:S(2)}) collective-permute-start(f32[2,2,128,128]{3,2,0,1:T(8,128)S(1)} %collective-permute-done.1), channel_id=1, source_target_pairs={{0,15},{1,0},{2,1},{3,2},{4,3},{5,4},{6,5},{7,6},{8,7},{9,8},{10,9... | collective-permute-start | bytes 786440 | tf_op jit(solution)/shard_map/ppermute | solution.py:69
  186.7 2.4 collective-permute-done.2
  189.1 1.9 collective-permute-start.4
  191.0 5.1 %collective-permute-start.5 = (f32[2,2,128,128]{3,2,0,1:T(8,128)S(1)}, f32[2,2,128,128]{3,2,0,1:T(8,128)S(1)}, u32[]{:S(2)}, u32[]{:S(2)}) collective-permute-start(f32[2,2,128,128]{3,2,0,1:T(8,128)S(1)} %collective-permute-done.3), channel_id=1, source_target_pairs={{0,15},{1,0},{2,1},{3,2},{4,3},{5,4},{6,5},{7,6},{8,7},{9,8},{10,9... | collective-permute-start | bytes 786440 | tf_op jit(solution)/shard_map/ppermute | solution.py:69
  196.5 2.1 collective-permute-done.4
  198.6 1.9 collective-permute-start.6
  200.5 0.5 broadcast_in_dim.2
  201.1 0.7 copy.15
  201.8 5.1 %collective-permute-start.7 = (f32[2,2,128,128]{3,2,0,1:T(8,128)S(1)}, f32[2,2,128,128]{3,2,0,1:T(8,128)S(1)}, u32[]{:S(2)}, u32[]{:S(2)}) collective-permute-start(f32[2,2,128,128]{3,2,0,1:T(8,128)S(1)} %collective-permute-done.5), channel_id=1, source_target_pairs={{0,15},{1,0},{2,1},{3,2},{4,3},{5,4},{6,5},{7,6},{8,7},{9,8},{10,9... | collective-permute-start | bytes 786440 | tf_op jit(solution)/shard_map/ppermute | solution.py:69
  207.0 1.0 collective-permute-done.6
  208.1 1.9 collective-permute-start.8
  210.0 0.8 collective-permute-done.7
  210.8 5.6 %collective-permute-start.9 = (f32[2,2,128,128]{3,2,0,1:T(8,128)S(1)}, f32[2,2,128,128]{3,2,0,1:T(8,128)S(1)}, u32[]{:S(2)}, u32[]{:S(2)}) collective-permute-start(f32[2,2,128,128]{3,2,0,1:T(8,128)S(1)} %collective-permute-done.7), channel_id=1, source_target_pairs={{0,15},{1,0},{2,1},{3,2},{4,3},{5,4},{6,5},{7,6},{8,7},{9,8},{10,9... | collective-permute-start | bytes 786440 | tf_op jit(solution)/shard_map/ppermute | solution.py:69
  216.5 1.9 collective-permute-done.8
  218.4 1.9 collective-permute-start.10
  220.4 1.0 collective-permute-done.9
  221.4 5.6 %collective-permute-start.11 = (f32[2,2,128,128]{3,2,0,1:T(8,128)S(1)}, f32[2,2,128,128]{3,2,0,1:T(8,128)S(1)}, u32[]{:S(2)}, u32[]{:S(2)}) collective-permute-start(f32[2,2,128,128]{3,2,0,1:T(8,128)S(1)} %collective-permute-done.9), channel_id=1, source_target_pairs={{0,15},{1,0},{2,1},{3,2},{4,3},{5,4},{6,5},{7,6},{8,7},{9,8},{10,9... | collective-permute-start | bytes 786440 | tf_op jit(solution)/shard_map/ppermute | solution.py:69
  227.0 2.8 %collective-permute-done.10 = f32[2,2,128,128]{3,2,0,1:T(8,128)S(1)} collective-permute-done((f32[2,2,128,128]{3,2,0,1:T(8,128)S(1)}, f32[2,2,128,128]{3,2,0,1:T(8,128)S(1)}, u32[]{:S(2)}, u32[]{:S(2)}) %collective-permute-start.10) | collective-permute-done | bytes 262176 | tf_op jit(solution)/shard_map/ppermute | solution.py:66
  229.8 1.9 collective-permute-start.12
  231.8 5.1 %collective-permute-start.13 = (f32[2,2,128,128]{3,2,0,1:T(8,128)S(1)}, f32[2,2,128,128]{3,2,0,1:T(8,128)S(1)}, u32[]{:S(2)}, u32[]{:S(2)}) collective-permute-start(f32[2,2,128,128]{3,2,0,1:T(8,128)S(1)} %collective-permute-done.11), channel_id=1, source_target_pairs={{0,15},{1,0},{2,1},{3,2},{4,3},{5,4},{6,5},{7,6},{8,7},{9,8},{10,9... | collective-permute-start | bytes 786440 | tf_op jit(solution)/shard_map/ppermute | solution.py:69
  237.0 2.3 collective-permute-done.12
  239.3 2.1 collective-permute-start.14
  241.5 7.2 %collective-permute-done.14 = f32[2,2,128,128]{3,2,0,1:T(8,128)S(1)} collective-permute-done((f32[2,2,128,128]{3,2,0,1:T(8,128)S(1)}, f32[2,2,128,128]{3,2,0,1:T(8,128)S(1)}, u32[]{:S(2)}, u32[]{:S(2)}) %collective-permute-start.14) | collective-permute-done | bytes 262176 | tf_op jit(solution)/shard_map/ppermute | solution.py:66
  248.8 1.8 fusion.5
  250.6 1.8 fusion.4
  252.5 1.8 fusion.7
  254.3 1.8 fusion.9
  256.2 0.7 copy.16
  (32 shorter events, 0.5 us)
Async XLA Ops:
  7.2 71.8 %copy-start.1 = (f32[2,2,128,128]{3,2,1,0:T(8,128)S(1)}, f32[2,2,128,128]{3,2,1,0:T(8,128)}, u32[]{:S(2)}) copy-start(f32[2,2,128,128]{3,2,1,0:T(8,128)} %param.7) | copy-start | bytes 786436
  7.2 67.7 %all-gather.2.cloned.1.call-start = ((), (), s32[]{:S(2)}) async-start(), calls=%async_computation.1 | async-start | bytes 2162688 | tf_op jit(solution)/shard_map/all_gather | solution.py:49
  8.8 160.3 %reduce-scatter.2.cloned.1.call-start = ((), (), s32[]{:S(2)}) async-start(), calls=%async_computation.2 | async-start | bytes 4456448 | tf_op jit(solution)/shard_map/reduce_scatter | solution.py:54
  169.1 31.9 %copy-start.2 = (f32[2,2,128,128]{3,2,0,1:T(8,128)S(1)}, f32[2,2,128,128]{3,2,0,1:T(8,128)}, u32[]{:S(2)}) copy-start(f32[2,2,128,128]{3,2,0,1:T(8,128)} %reduce-scatter.2.cloned.1.call-done) | copy-start | bytes 786436
  169.1 10.6 %collective-permute-start = (f32[2,2,128,128]{3,2,0,1:T(8,128)}, f32[2,2,128,128]{3,2,0,1:T(8,128)S(1)}, u32[]{:S(2)}, u32[]{:S(2)}) collective-permute-start(f32[2,2,128,128]{3,2,0,1:T(8,128)} %reduce-scatter.2.cloned.1.call-done), channel_id=1, source_target_pairs={{0,1},{1,2},{2,3},{3,4},{4,5},{5,6},{6,7},{7,8},{8,9},{9,10},{10,1... | collective-permute-start | bytes 786440 | tf_op jit(solution)/shard_map/ppermute | solution.py:66
  171.6 10.0 %collective-permute-start.1 = (f32[2,2,128,128]{3,2,0,1:T(8,128)}, f32[2,2,128,128]{3,2,0,1:T(8,128)S(1)}, u32[]{:S(2)}, u32[]{:S(2)}) collective-permute-start(f32[2,2,128,128]{3,2,0,1:T(8,128)} %reduce-scatter.2.cloned.1.call-done), channel_id=1, source_target_pairs={{0,15},{1,0},{2,1},{3,2},{4,3},{5,4},{6,5},{7,6},{8,7},{9,8},{10,9... | collective-permute-start | bytes 786440 | tf_op jit(solution)/shard_map/ppermute | solution.py:69
  179.7 9.5 %collective-permute-start.2 = (f32[2,2,128,128]{3,2,0,1:T(8,128)S(1)}, f32[2,2,128,128]{3,2,0,1:T(8,128)S(1)}, u32[]{:S(2)}, u32[]{:S(2)}) collective-permute-start(f32[2,2,128,128]{3,2,0,1:T(8,128)S(1)} %collective-permute-done), channel_id=1, source_target_pairs={{0,1},{1,2},{2,3},{3,4},{4,5},{5,6},{6,7},{7,8},{8,9},{9,10},{10,1... | collective-permute-start | bytes 786440 | tf_op jit(solution)/shard_map/ppermute | solution.py:66
  181.6 9.5 %collective-permute-start.3 = (f32[2,2,128,128]{3,2,0,1:T(8,128)S(1)}, f32[2,2,128,128]{3,2,0,1:T(8,128)S(1)}, u32[]{:S(2)}, u32[]{:S(2)}) collective-permute-start(f32[2,2,128,128]{3,2,0,1:T(8,128)S(1)} %collective-permute-done.1), channel_id=1, source_target_pairs={{0,15},{1,0},{2,1},{3,2},{4,3},{5,4},{6,5},{7,6},{8,7},{9,8},{10,9... | collective-permute-start | bytes 786440 | tf_op jit(solution)/shard_map/ppermute | solution.py:69
  189.1 9.5 %collective-permute-start.4 = (f32[2,2,128,128]{3,2,0,1:T(8,128)S(1)}, f32[2,2,128,128]{3,2,0,1:T(8,128)S(1)}, u32[]{:S(2)}, u32[]{:S(2)}) collective-permute-start(f32[2,2,128,128]{3,2,0,1:T(8,128)S(1)} %collective-permute-done.2), channel_id=1, source_target_pairs={{0,1},{1,2},{2,3},{3,4},{4,5},{5,6},{6,7},{7,8},{8,9},{9,10},{10,1... | collective-permute-start | bytes 786440 | tf_op jit(solution)/shard_map/ppermute | solution.py:66
  191.0 10.8 %collective-permute-start.5 = (f32[2,2,128,128]{3,2,0,1:T(8,128)S(1)}, f32[2,2,128,128]{3,2,0,1:T(8,128)S(1)}, u32[]{:S(2)}, u32[]{:S(2)}) collective-permute-start(f32[2,2,128,128]{3,2,0,1:T(8,128)S(1)} %collective-permute-done.3), channel_id=1, source_target_pairs={{0,15},{1,0},{2,1},{3,2},{4,3},{5,4},{6,5},{7,6},{8,7},{9,8},{10,9... | collective-permute-start | bytes 786440 | tf_op jit(solution)/shard_map/ppermute | solution.py:69
  198.6 9.5 %collective-permute-start.6 = (f32[2,2,128,128]{3,2,0,1:T(8,128)S(1)}, f32[2,2,128,128]{3,2,0,1:T(8,128)S(1)}, u32[]{:S(2)}, u32[]{:S(2)}) collective-permute-start(f32[2,2,128,128]{3,2,0,1:T(8,128)S(1)} %collective-permute-done.4), channel_id=1, source_target_pairs={{0,1},{1,2},{2,3},{3,4},{4,5},{5,6},{6,7},{7,8},{8,9},{9,10},{10,1... | collective-permute-start | bytes 786440 | tf_op jit(solution)/shard_map/ppermute | solution.py:66
  201.1 47.8 %copy-start = (f32[1,2,2048,128]{3,2,1,0:T(8,128)S(1)}, f32[1,2,2048,128]{3,2,1,0:T(8,128)}, u32[]{:S(2)}) copy-start(f32[1,2,2048,128]{3,2,1,0:T(8,128)} %param.11) | copy-start | bytes 6291460
  201.8 9.0 %collective-permute-start.7 = (f32[2,2,128,128]{3,2,0,1:T(8,128)S(1)}, f32[2,2,128,128]{3,2,0,1:T(8,128)S(1)}, u32[]{:S(2)}, u32[]{:S(2)}) collective-permute-start(f32[2,2,128,128]{3,2,0,1:T(8,128)S(1)} %collective-permute-done.5), channel_id=1, source_target_pairs={{0,15},{1,0},{2,1},{3,2},{4,3},{5,4},{6,5},{7,6},{8,7},{9,8},{10,9... | collective-permute-start | bytes 786440 | tf_op jit(solution)/shard_map/ppermute | solution.py:69
  208.1 10.3 %collective-permute-start.8 = (f32[2,2,128,128]{3,2,0,1:T(8,128)S(1)}, f32[2,2,128,128]{3,2,0,1:T(8,128)S(1)}, u32[]{:S(2)}, u32[]{:S(2)}) collective-permute-start(f32[2,2,128,128]{3,2,0,1:T(8,128)S(1)} %collective-permute-done.6), channel_id=1, source_target_pairs={{0,1},{1,2},{2,3},{3,4},{4,5},{5,6},{6,7},{7,8},{8,9},{9,10},{10,1... | collective-permute-start | bytes 786440 | tf_op jit(solution)/shard_map/ppermute | solution.py:66
  210.8 10.5 %collective-permute-start.9 = (f32[2,2,128,128]{3,2,0,1:T(8,128)S(1)}, f32[2,2,128,128]{3,2,0,1:T(8,128)S(1)}, u32[]{:S(2)}, u32[]{:S(2)}) collective-permute-start(f32[2,2,128,128]{3,2,0,1:T(8,128)S(1)} %collective-permute-done.7), channel_id=1, source_target_pairs={{0,15},{1,0},{2,1},{3,2},{4,3},{5,4},{6,5},{7,6},{8,7},{9,8},{10,9... | collective-permute-start | bytes 786440 | tf_op jit(solution)/shard_map/ppermute | solution.py:69
  218.4 11.5 %collective-permute-start.10 = (f32[2,2,128,128]{3,2,0,1:T(8,128)S(1)}, f32[2,2,128,128]{3,2,0,1:T(8,128)S(1)}, u32[]{:S(2)}, u32[]{:S(2)}) collective-permute-start(f32[2,2,128,128]{3,2,0,1:T(8,128)S(1)} %collective-permute-done.8), channel_id=1, source_target_pairs={{0,1},{1,2},{2,3},{3,4},{4,5},{5,6},{6,7},{7,8},{8,9},{9,10},{10,1... | collective-permute-start | bytes 786440 | tf_op jit(solution)/shard_map/ppermute | solution.py:66
  221.4 10.5 %collective-permute-start.11 = (f32[2,2,128,128]{3,2,0,1:T(8,128)S(1)}, f32[2,2,128,128]{3,2,0,1:T(8,128)S(1)}, u32[]{:S(2)}, u32[]{:S(2)}) collective-permute-start(f32[2,2,128,128]{3,2,0,1:T(8,128)S(1)} %collective-permute-done.9), channel_id=1, source_target_pairs={{0,15},{1,0},{2,1},{3,2},{4,3},{5,4},{6,5},{7,6},{8,7},{9,8},{10,9... | collective-permute-start | bytes 786440 | tf_op jit(solution)/shard_map/ppermute | solution.py:69
  229.8 9.5 %collective-permute-start.12 = (f32[2,2,128,128]{3,2,0,1:T(8,128)S(1)}, f32[2,2,128,128]{3,2,0,1:T(8,128)S(1)}, u32[]{:S(2)}, u32[]{:S(2)}) collective-permute-start(f32[2,2,128,128]{3,2,0,1:T(8,128)S(1)} %collective-permute-done.10), channel_id=1, source_target_pairs={{0,1},{1,2},{2,3},{3,4},{4,5},{5,6},{6,7},{7,8},{8,9},{9,10},{10,1... | collective-permute-start | bytes 786440 | tf_op jit(solution)/shard_map/ppermute | solution.py:66
  231.8 9.6 %collective-permute-start.13 = (f32[2,2,128,128]{3,2,0,1:T(8,128)S(1)}, f32[2,2,128,128]{3,2,0,1:T(8,128)S(1)}, u32[]{:S(2)}, u32[]{:S(2)}) collective-permute-start(f32[2,2,128,128]{3,2,0,1:T(8,128)S(1)} %collective-permute-done.11), channel_id=1, source_target_pairs={{0,15},{1,0},{2,1},{3,2},{4,3},{5,4},{6,5},{7,6},{8,7},{9,8},{10,9... | collective-permute-start | bytes 786440 | tf_op jit(solution)/shard_map/ppermute | solution.py:69
  239.3 9.5 %collective-permute-start.14 = (f32[2,2,128,128]{3,2,0,1:T(8,128)S(1)}, f32[2,2,128,128]{3,2,0,1:T(8,128)S(1)}, u32[]{:S(2)}, u32[]{:S(2)}) collective-permute-start(f32[2,2,128,128]{3,2,0,1:T(8,128)S(1)} %collective-permute-done.12), channel_id=1, source_target_pairs={{0,1},{1,2},{2,3},{3,4},{4,5},{5,6},{6,7},{7,8},{8,9},{9,10},{10,1... | collective-permute-start | bytes 786440 | tf_op jit(solution)/shard_map/ppermute | solution.py:66
Sparse Core Ops, SparseCore 0:
  11.7 63.0 all-gather.1
  88.8 80.2 reduce-scatter.1
